TPU v7x, 256 devices: a whole 4x4x8 slice. The times are simulated.
256 devices in a mesh: replica: 32 (over z, x), tensor: 8 (over y, core).
Axes of the slice: x: 4, y: 4, z: 8, core: 2. Of those that a mesh axis runs over, the one named last changes fastest.
Arguments:
- momentum: float32 [32, 256, 27648], P('replica', None, 'tensor'), may hold values from -6 to 6
- grads: bfloat16 [32, 2, 256, 27648], P('replica', None, None, 'tensor'), may hold values from -1500 to 1500, as said below
Outputs:
- new_momentum: float32 [32, 256, 27648], P('replica', None, 'tensor')
- update: bfloat16 [256, 27648], P(None, 'tensor')
Inputs may be any that keep to these rules, and one draw needn't show every extreme that they name: `grads`: gradients of each replica and step; magnitudes vary over rows, hidden units, replicas and steps.
All inputs are finite; a program needn't handle non-finite values.
Results may differ from a plain program's by a relative error of at most 0.001.
Values sent between devices are 32-bit elements; how exact they have to be, the bound alone decides.
A program may use at most 128 MiB of HBM per device.

v0:
```python
import math

import jax
import jax.numpy as jnp
from jax import lax
from jax.sharding import PartitionSpec as P

TILE = 32
BAND = 8
STEPS = 2


HIGH = lax.Precision.HIGHEST
BETA = 0.9
CLIP = 1.0
EPS = 1e-06


def band_matrix():
    freq = jnp.arange(BAND, dtype=jnp.float32)[:, None]
    place = jnp.arange(TILE, dtype=jnp.float32)[None, :]
    weight = jnp.where(freq == 0, math.sqrt(1.0 / TILE), math.sqrt(2.0 / TILE))
    return weight * jnp.cos(math.pi * (2.0 * place + 1.0) * freq / (2.0 * TILE))


def encode(field, low_band):
    row_count, col_count = field.shape
    tiles = field.reshape(row_count // TILE, TILE, col_count)
    half = jnp.einsum("kn,anf->akf", low_band, tiles, precision=HIGH)
    half = half.reshape(row_count // TILE, BAND, col_count // TILE, TILE)
    whole = jnp.einsum("ln,akfn->akfl", low_band, half, precision=HIGH)
    return whole.reshape(row_count // TILE * BAND, col_count // TILE * BAND)


def decode(band, low_band, row_count, col_count):
    blocks = band.reshape(row_count // TILE, BAND, col_count // TILE, BAND)
    half = jnp.einsum("ln,akfl->akfn", low_band, blocks, precision=HIGH)
    half = half.reshape(row_count // TILE, BAND, col_count)
    whole = jnp.einsum("kn,akf->anf", low_band, half, precision=HIGH)
    return whole.reshape(row_count, col_count)


def per_device(momentum, grads):
    low_band = band_matrix()
    row_count, col_count = (momentum.shape[1], momentum.shape[2])
    count = float(lax.axis_size("replica") * lax.axis_size("tensor") * row_count * col_count)
    state = momentum[0]
    local_sq = [jnp.sum(jnp.square(grads[0, step].astype(jnp.float32))) for step in range(STEPS)]
    update_sum = jnp.zeros((row_count, col_count), jnp.float32)
    for step in range(STEPS):
        total = lax.psum(local_sq[step], ("replica", "tensor"))
        scale = jnp.minimum(1.0, CLIP / jnp.sqrt(total / count + EPS))
        state = BETA * state + scale * grads[0, step].astype(jnp.float32)
        band = encode(state, low_band)
        summed = lax.psum(band, "replica")
        update_sum = update_sum + decode(summed, low_band, row_count, col_count)
        state = state - decode(band, low_band, row_count, col_count)
    return (state[None], update_sum.astype(jnp.bfloat16))


def solution(mesh):
    in_specs = (P("replica", None, "tensor"), P("replica", None, None, "tensor"))
    out_specs = (P("replica", None, "tensor"), P(None, "tensor"))
    return jax.shard_map(
        per_device, mesh=mesh, in_specs=in_specs, out_specs=out_specs, check_vma=False
    )
```

profile of v0, /device:TPU:32, one launch (start us, length us, event | category | flops | bytes accessed | tf_op | source)
XLA Modules:
  0.0 340.3 jit_solution(9129682164670827255)
XLA Ops:
  7.2 3.7 %fusion.1 = (f32[]{:T(128)}, f32[]{:T(128)}) fusion(bf16[1,2,256,3456]{3,2,1,0:T(8,128)(2,1)} %param.3), kind=kLoop, calls=%fused_computation.8 | loop fusion | flops 5308414 | bytes 3538952 | tf_op jit(solution)/shard_map/reduce_sum | solution.py:48
  10.9 79.8 %all-reduce = (f32[]{:T(128)}, f32[]{:T(128)}) all-reduce(f32[]{:T(128)} %get-tuple-element.3, f32[]{:T(128)} %get-tuple-element.2), channel_id=1, replica_groups=mesh['replica'=32,'tensor'=8] {'replica','tensor'}, use_global_device_ids=true, to_apply=%region_3.4 | all-reduce | flops 2 | bytes 16 | tf_op jit(solution)/shard_map/psum | solution.py:51
  94.1 2.3 convert_multiply_fusion.2
  96.8 2.9 convolution_bitcast_fusion.1
  99.7 3.8 %reshape.113 = f32[8,8,108,32]{3,2,1,0:T(8,128)} reshape(f32[8,8,3456]{2,1,0:T(8,128)} %convolution_bitcast_fusion.1) | data formatting | bytes 1769472 | tf_op jit(solution)/shard_map/reshape | solution.py:30
  103.5 8.2 %fusion.19 = f32[8,8,108,8]{2,3,1,0:T(8,128)S(1)} fusion(f32[8,8,108,32]{3,2,1,0:T(8,128)} %reshape.113, f32[32]{0:T(128)S(1)} %add_multiply_fusion, f32[8]{0:T(128)S(1)} %compare_select_fusion), kind=kOutput, calls=%fused_computation.30 | convolution fusion | flops 21234432 | bytes 1106080 | tf_op jit(solution)/shard_map/ln,akfn->akfl/dot_general | solution.py:31
  112.4 7.7 %fusion.17 = f32[8,8,108,32]{3,2,1,0:T(8,128)} fusion(f32[8,8,108,8]{2,3,1,0:T(8,128)S(1)} %fusion.19, f32[32]{0:T(128)S(1)} %add_multiply_fusion, f32[8]{0:T(128)S(1)} %compare_select_fusion), kind=kOutput, calls=%fused_computation.28 | convolution fusion | flops 21234432 | bytes 1106080 | tf_op jit(solution)/shard_map/ln,akfl->akfn/dot_general | solution.py:37
  120.1 3.7 %reshape.114 = f32[8,8,3456]{2,1,0:T(8,128)} reshape(f32[8,8,108,32]{3,2,1,0:T(8,128)} %fusion.17) | data formatting | bytes 1769472 | tf_op jit(solution)/shard_map/reshape | solution.py:38
  123.8 4.4 %fusion.27 = f32[8,3456,32]{1,2,0:T(8,128)S(1)} fusion(f32[8,8,3456]{2,1,0:T(8,128)} %reshape.114, f32[32]{0:T(128)S(1)} %add_multiply_fusion, f32[8]{0:T(128)S(1)} %compare_select_fusion), kind=kOutput, calls=%fused_computation.38 | convolution fusion | flops 84935424 | bytes 4423840 | tf_op jit(solution)/shard_map/kn,akf->anf/dot_general | solution.py:39
  128.2 1.8 copy-done.2
  130.0 3.3 convolution_bitcast_fusion
  133.3 4.0 %reshape.116 = f32[8,8,108,32]{3,2,1,0:T(8,128)} reshape(f32[8,8,3456]{2,1,0:T(8,128)} %convolution_bitcast_fusion) | data formatting | bytes 1769472 | tf_op jit(solution)/shard_map/reshape | solution.py:30
  137.3 8.2 %fusion.15 = f32[8,8,108,8]{2,3,1,0:T(8,128)S(1)} fusion(f32[8,8,108,32]{3,2,1,0:T(8,128)} %reshape.116, f32[32]{0:T(128)S(1)} %add_multiply_fusion, f32[8]{0:T(128)S(1)} %compare_select_fusion), kind=kOutput, calls=%fused_computation.26 | convolution fusion | flops 21234432 | bytes 1106080 | tf_op jit(solution)/shard_map/ln,akfn->akfl/dot_general | solution.py:31
  145.6 7.7 %fusion.13 = f32[8,8,108,32]{3,2,1,0:T(8,128)} fusion(f32[8,8,108,8]{2,3,1,0:T(8,128)S(1)} %fusion.15, f32[32]{0:T(128)S(1)} %add_multiply_fusion, f32[8]{0:T(128)S(1)} %compare_select_fusion), kind=kOutput, calls=%fused_computation.24 | convolution fusion | flops 21234432 | bytes 1106080 | tf_op jit(solution)/shard_map/ln,akfl->akfn/dot_general | solution.py:37
  154.0 3.8 %reshape.117 = f32[8,8,3456]{2,1,0:T(8,128)} reshape(f32[8,8,108,32]{3,2,1,0:T(8,128)} %fusion.13) | data formatting | bytes 1769472 | tf_op jit(solution)/shard_map/reshape | solution.py:38
  157.8 4.4 %fusion.24 = f32[8,3456,32]{1,2,0:T(8,128)S(1)} fusion(f32[8,8,3456]{2,1,0:T(8,128)} %reshape.117, f32[32]{0:T(128)S(1)} %add_multiply_fusion, f32[8]{0:T(128)S(1)} %compare_select_fusion), kind=kOutput, calls=%fused_computation.35 | convolution fusion | flops 84935424 | bytes 4423840 | tf_op jit(solution)/shard_map/kn,akf->anf/dot_general | solution.py:39
  162.3 5.5 %bitcast_subtract_fusion = f32[1,256,3456]{2,1,0:T(8,128)} fusion(f32[8,3456,32]{1,2,0:T(8,128)S(1)} %fusion.24, f32[8,3456,32]{1,2,0:T(8,128)S(1)} %copy-done.3, bf16[1,2,256,3456]{3,2,1,0:T(8,128)(2,1)S(1)} %copy-done.1, f32[]{:T(128)S(6)} %min.6, f32[]{:T(128)S(6)} %min.7, f32[1,256,3456]{2,1,0:T(8,128)} %param.2), kind=kLoop, calls=%fused_computation.10 | loop fusion | flops 8847360 | bytes 17694728 | tf_op jit(solution)/shard_map/sub | solution.py:57
  167.7 132.0 %all-reduce.4.cloned.1.call-done = (f32[8,8,108,8]{2,3,1,0:T(8,128)}, f32[8,8,108,8]{2,3,1,0:T(8,128)}) async-done(((f32[8,8,108,8]{2,3,1,0:T(8,128)}, f32[8,8,108,8]{2,3,1,0:T(8,128)}), (f32[8,8,108,8]{2,3,1,0:T(8,128)}, f32[8,8,108,8]{2,3,1,0:T(8,128)})) %all-reduce.4.cloned.1.call-update) | async-done | bytes 442384 | tf_op jit(solution)/shard_map/psum | solution.py:55
  299.7 8.6 %fusion.11 = f32[8,8,108,32]{3,2,1,0:T(8,128)} fusion(f32[8,8,108,8]{2,3,1,0:T(8,128)} %get-tuple-element.6, f32[32]{0:T(128)S(1)} %add_multiply_fusion, f32[8]{0:T(128)S(1)} %compare_select_fusion), kind=kOutput, calls=%fused_computation.22 | convolution fusion | flops 21234432 | bytes 1106080 | tf_op jit(solution)/shard_map/ln,akfl->akfn/dot_general | solution.py:37
  308.3 3.7 %reshape.121 = f32[8,8,3456]{2,1,0:T(8,128)} reshape(f32[8,8,108,32]{3,2,1,0:T(8,128)} %fusion.11) | data formatting | bytes 1769472 | tf_op jit(solution)/shard_map/reshape | solution.py:38
  312.0 4.3 %fusion.22 = f32[8,3456,32]{1,2,0:T(8,128)S(1)} fusion(f32[8,8,3456]{2,1,0:T(8,128)} %reshape.121, f32[32]{0:T(128)S(1)} %add_multiply_fusion, f32[8]{0:T(128)S(1)} %compare_select_fusion), kind=kOutput, calls=%fused_computation.33 | convolution fusion | flops 84935424 | bytes 4423840 | tf_op jit(solution)/shard_map/kn,akf->anf/dot_general | solution.py:39
  316.3 7.7 %fusion.9 = f32[8,8,108,32]{3,2,1,0:T(8,128)} fusion(f32[8,8,108,8]{2,3,1,0:T(8,128)S(1)} %copy-done.8, f32[32]{0:T(128)S(1)} %add_multiply_fusion, f32[8]{0:T(128)S(1)} %compare_select_fusion), kind=kOutput, calls=%fused_computation.20 | convolution fusion | flops 21234432 | bytes 1106080 | tf_op jit(solution)/shard_map/ln,akfl->akfn/dot_general | solution.py:37
  324.0 3.7 %reshape.124 = f32[8,8,3456]{2,1,0:T(8,128)} reshape(f32[8,8,108,32]{3,2,1,0:T(8,128)} %fusion.9) | data formatting | bytes 1769472 | tf_op jit(solution)/shard_map/reshape | solution.py:38
  327.7 5.5 %fusion = bf16[8,3456,32]{1,2,0:T(8,128)(2,1)} fusion(f32[8,3456,32]{1,2,0:T(8,128)S(1)} %fusion.22, f32[8,8,3456]{2,1,0:T(8,128)} %reshape.124, f32[32]{0:T(128)S(1)} %add_multiply_fusion, f32[8]{0:T(128)S(1)} %compare_select_fusion), kind=kOutput, calls=%fused_computation.1 | convolution fusion | flops 86704896 | bytes 6193312 | tf_op jit(solution)/shard_map/kn,akf->anf/dot_general | solution.py:39
  (23 shorter events, 3.8 us)
Async XLA Ops:
  7.2 84.9 %copy-start.5 = (f32[1,256,3456]{2,1,0:T(8,128)S(1)}, f32[1,256,3456]{2,1,0:T(8,128)}, u32[]{:S(2)}) copy-start(f32[1,256,3456]{2,1,0:T(8,128)} %param.2) | copy-start | bytes 10616836
  92.1 2.0 copy-start
  111.7 0.7 copy-start.6
  123.8 6.2 %copy-start.4 = (f32[1,1,256,3456]{3,2,1,0:T(8,128)S(1)}, f32[1,1,256,3456]{3,2,1,0:T(8,128)}, u32[]{:S(2)}) copy-start(f32[1,1,256,3456]{3,2,1,0:T(8,128)} %get-tuple-element.9) | copy-start | bytes 10616836
  128.2 1.8 copy-start.2
  145.6 7.7 %copy-start.7 = (f32[8,8,108,8]{2,3,1,0:T(8,128)}, f32[8,8,108,8]{2,3,1,0:T(8,128)S(1)}, u32[]{:S(2)}) copy-start(f32[8,8,108,8]{2,3,1,0:T(8,128)S(1)} %fusion.15) | copy-start | bytes 663556
  153.3 146.4 %all-reduce.4.cloned.1.call-start = ((), (), s32[]{:S(2)}) async-start(), calls=%async_computation | async-start | bytes 1048576 | tf_op jit(solution)/shard_map/psum | solution.py:55
  154.0 8.2 %copy-start.1 = (bf16[1,2,256,3456]{3,2,1,0:T(8,128)(2,1)S(1)}, bf16[1,2,256,3456]{3,2,1,0:T(8,128)(2,1)}, u32[]{:S(2)}) copy-start(bf16[1,2,256,3456]{3,2,1,0:T(8,128)(2,1)} %param.3) | copy-start | bytes 10616836
  157.8 4.4 %copy-start.3 = (f32[8,3456,32]{1,2,0:T(8,128)S(1)}, f32[8,3456,32]{1,2,0:T(8,128)}, u32[]{:S(2)}) copy-start(f32[8,3456,32]{1,2,0:T(8,128)} %copy-done.2) | copy-start | bytes 10616836
  312.0 4.3 %copy-start.8 = (f32[8,8,108,8]{2,3,1,0:T(8,128)S(1)}, f32[8,8,108,8]{2,3,1,0:T(8,128)}, u32[]{:S(2)}) copy-start(f32[8,8,108,8]{2,3,1,0:T(8,128)} %get-tuple-element.7) | copy-start | bytes 663556
Sparse Core Ops, SparseCore 0:
  157.5 142.0 all-reduce.3
where the time goes:
time: 347 us; the launch traced here: 340 us
  waiting for transfers between devices  133 us (38%)
  blocking collectives  79.8 us (23%)
  matrix products  73 us (21%)
  local copies, waits for them, and re-layouts  26.8 us (8%)
  between operations  15.8 us (5%)
  other arithmetic  12.1 us (3%)
    psum x1, waiting for transfers between devices, per_device(): summed = lax.psum(band, 'replica')  132 us
    psum x1, blocking collectives, per_device(): total = lax.psum(local_sq[step], ('replica', 'tensor'))  79.8 us
    dot_general x4, matrix products, decode(): half = jnp.einsum('ln,akfl->akfn', low_band, blocks, precision=HIGH)  31.8 us
    dot_general x4, matrix products, decode(): whole = jnp.einsum('kn,akf->anf', low_band, half, precision=HIGH)  18.6 us
    dot_general x2, matrix products, encode(): whole = jnp.einsum('ln,akfn->akfl', low_band, half, precision=HIGH)  16.5 us
    reshape x4, local copies, waits for them, and re-layouts, decode(): half = half.reshape(row_count // TILE, BAND, col_count)  14.8 us
    reshape x2, local copies, waits for them, and re-layouts, encode(): half = half.reshape(row_count // TILE, BAND, col_count // TILE, TILE)  7.83 us
  transfers between devices with their start and end apart: 1, of which 1 were waited for; matrix products, arithmetic and copies ran while one was open for 4% of the time, Pallas kernels for 0%

commit v1 on v0

v1 whole, which is shorter than its diff:
```python
import functools
import math

import jax
import jax.numpy as jnp
import ml_dtypes
import numpy as np
from jax import lax
from jax.experimental import pallas as pl
from jax.experimental.pallas import tpu as pltpu
from jax.sharding import PartitionSpec as P

TILE = 32
BAND = 8
STEPS = 2
BETA = 0.9
CLIP = 1.0
EPS = 1e-06

MESH = pl.DeviceIdType.MESH
F32 = jnp.float32
BF16 = jnp.bfloat16

REP = 32
TEN = 8
ROWS = 256
COLS = 3456
GCOL = 512
GROUPS = 7
LAST = COLS - (GROUPS - 1) * GCOL
BROW = ROWS // TILE * BAND
BCOL = GCOL // TILE * BAND
QUART = 16
PIECES = GROUPS * (BROW // QUART)


def tables():
    freq = np.arange(BAND, dtype=np.float64)[:, None]
    place = np.arange(TILE, dtype=np.float64)[None, :]
    weight = np.where(freq == 0, math.sqrt(1.0 / TILE), math.sqrt(2.0 / TILE))
    low = weight * np.cos(math.pi * (2.0 * place + 1.0) * freq / (2.0 * TILE))

    def split(a):
        hi = a.astype(ml_dtypes.bfloat16)
        lo = (a - hi.astype(np.float64)).astype(ml_dtypes.bfloat16)
        return hi, lo

    col_hi, col_lo = split(np.kron(np.eye(GCOL // TILE), low))
    row_hi, row_lo = split(np.kron(np.eye(ROWS // TILE), low))
    w_enc = np.concatenate([col_hi.T, col_lo.T], axis=1)
    l_enc = np.concatenate([row_hi, row_lo], axis=0)
    w_dec = np.concatenate([col_hi, col_hi, col_lo], axis=0)
    l_dec = np.concatenate([row_hi.T, row_hi.T, row_lo.T], axis=1)
    return w_enc, l_enc, w_dec, l_dec


def halves(a):
    hi = a.astype(BF16)
    return hi, (a - hi.astype(F32)).astype(BF16)


def dot(a, b):
    return jnp.dot(a, b, preferred_element_type=F32)


def decode_group(band, w_dec, l_dec):
    hi, lo = halves(band)
    wide = dot(jnp.concatenate([hi, lo, hi], axis=1), w_dec)
    hi, lo = halves(wide)
    return dot(l_dec, jnp.concatenate([hi, lo, hi], axis=0))


def sync_kernel(
    m_hbm, g_hbm, wenc_hbm, lenc_hbm, wdec_hbm, ldec_hbm,
    nm, summed, wdec, ldec,
    m_v, g_v, wenc, lenc, enc, band, band2, sq1, sq2, rbuf, abuf, scales,
    g_sem, m_sem, c_sem, s1_send, s1_recv, s2_send, s2_recv, r_send, r_recv, a_send, a_recv,
):
    rep = lax.axis_index("replica")
    ten = lax.axis_index("tensor")

    barrier = pltpu.get_barrier_semaphore()

    def greet_tensor(d, _):
        pl.semaphore_signal(barrier, inc=1, device_id={"tensor": lax.rem(ten + d, TEN)}, device_id_type=MESH)
        return 0

    def greet_replica(d, _):
        pl.semaphore_signal(barrier, inc=1, device_id={"replica": lax.rem(rep + d, REP)}, device_id_type=MESH)
        return 0

    def grad_copy(g, width):
        return pltpu.make_async_copy(
            g_hbm.at[0, :, :, pl.ds(g * GCOL, width)], g_v.at[g, :, :, pl.ds(0, width)], g_sem.at[g]
        )

    def mom_copy(g, width):
        return pltpu.make_async_copy(
            m_hbm.at[0, :, pl.ds(g * GCOL, width)], m_v.at[g, :, pl.ds(0, width)], m_sem.at[g]
        )

    widths = [GCOL] * (GROUPS - 1) + [LAST]
    for g in range(GROUPS):
        grad_copy(g, widths[g]).start()
    consts = [
        pltpu.make_async_copy(src, dst, c_sem.at[i])
        for i, (src, dst) in enumerate(((wenc_hbm, wenc), (lenc_hbm, lenc), (wdec_hbm, wdec), (ldec_hbm, ldec)))
    ]
    for copy in consts:
        copy.start()
    for g in range(GROUPS):
        mom_copy(g, widths[g]).start()

    lax.fori_loop(1, TEN, greet_tensor, 0)
    lax.fori_loop(1, REP, greet_replica, 0)

    m_v[GROUPS - 1, :, LAST:] = jnp.zeros((ROWS, GCOL - LAST), F32)
    g_v[GROUPS - 1, :, :, LAST:] = jnp.zeros((STEPS, ROWS, GCOL - LAST), BF16)

    def squares(g, sums):
        def rows(i, sums):
            at = pl.ds(pl.multiple_of(i * 16, 16), 16)
            x0 = g_v[g, 0, at, :].astype(F32)
            x1 = g_v[g, 1, at, :].astype(F32)
            return sums[0] + x0 * x0, sums[1] + x1 * x1

        return lax.fori_loop(0, ROWS // 16, rows, sums, unroll=4)

    sums = (jnp.zeros((16, GCOL), F32), jnp.zeros((16, GCOL), F32))

    def waited(g, sums):
        grad_copy(g, GCOL).wait()
        return squares(g, sums)

    sums = lax.fori_loop(0, GROUPS - 1, waited, sums)
    grad_copy(GROUPS - 1, LAST).wait()
    sums = squares(GROUPS - 1, sums)

    def lanes(x):
        x = jnp.sum(x, axis=0, keepdims=True)
        return x[:, :128] + x[:, 128:256] + x[:, 256:384] + x[:, 384:]

    sq1[ten] = jnp.concatenate([lanes(sums[0]), lanes(sums[1])], axis=0)
    pl.semaphore_wait(barrier, TEN - 1 + REP - 1)

    def send_tensor(d, _):
        pltpu.make_async_remote_copy(
            src_ref=sq1.at[ten], dst_ref=sq1.at[ten], send_sem=s1_send, recv_sem=s1_recv,
            device_id={"tensor": lax.rem(ten + d, TEN)}, device_id_type=MESH,
        ).start()
        return 0

    lax.fori_loop(1, TEN, send_tensor, 0)

    def drain(buf, count, send, recv):
        part = buf.at[pl.ds(0, count)]
        if send is not None:
            pltpu.make_async_copy(part, part, send).wait()
        if recv is not None:
            pltpu.make_async_copy(part, part, recv).wait()

    def encode_group(g):
        m_hi, m_lo = halves(m_v[g])
        w = wenc[...]
        part = dot(m_hi, w) + dot(m_lo, w)
        cols = [part]
        for s in range(STEPS):
            cols.append(dot(g_v[g, s], w))
        wide = jnp.concatenate([c[:, :BCOL] + c[:, BCOL:] for c in cols], axis=1)
        hi, lo = halves(wide)
        first = dot(lenc[...], hi)
        e = first[:BROW] + first[BROW:] + dot(lenc[:BROW], lo)
        for i in range(STEPS + 1):
            enc[g, i] = e[:, i * BCOL:(i + 1) * BCOL]

    def encode_waited(g, _):
        mom_copy(g, GCOL).wait()
        encode_group(g)
        return 0

    consts[0].wait()
    consts[1].wait()
    lax.fori_loop(0, 2, encode_waited, 0)

    drain(sq1, TEN - 1, s1_send, s1_recv)
    sq2[rep] = jnp.sum(sq1[...], axis=0)

    def send_replica(d, _):
        pltpu.make_async_remote_copy(
            src_ref=sq2.at[rep], dst_ref=sq2.at[rep], send_sem=s2_send, recv_sem=s2_recv,
            device_id={"replica": lax.rem(rep + d, REP)}, device_id_type=MESH,
        ).start()
        return 0

    lax.fori_loop(1, REP, send_replica, 0)

    lax.fori_loop(2, GROUPS - 1, encode_waited, 0)
    mom_copy(GROUPS - 1, LAST).wait()
    encode_group(GROUPS - 1)

    drain(sq2, REP - 1, s2_send, s2_recv)
    total = jnp.sum(jnp.sum(sq2[...], axis=0), axis=1, keepdims=True)
    total = jnp.broadcast_to(total, (STEPS, 128))
    count = float(REP * ROWS * TEN * COLS)
    scale = jnp.minimum(1.0, CLIP / jnp.sqrt(total / count + EPS))
    scales[...] = scale
    s0, s1 = scale[0:1], scale[1:2]

    for g in range(GROUPS):
        first = BETA * enc[g, 0] + s0 * enc[g, 1]
        second = s1 * enc[g, 2]
        band[pl.ds(4 * g, 4)] = (first + second).reshape(4, QUART, BCOL)
        band2[g] = BETA * first + second

    def send_piece(d, _):
        peer = lax.rem(rep + d, REP)

        @pl.when(peer < PIECES)
        def _():
            pltpu.make_async_remote_copy(
                src_ref=band.at[peer], dst_ref=rbuf.at[rep], send_sem=r_send, recv_sem=r_recv,
                device_id={"replica": peer}, device_id_type=MESH,
            ).start()

        return 0

    lax.fori_loop(1, REP, send_piece, 0)

    consts[2].wait()
    consts[3].wait()

    def momentum_group(g, _):
        sc = scales[...]
        t0, t1 = sc[0:1, 0:1], sc[1:2, 0:1]
        low = decode_group(band2[g], wdec[...], ldec[...])
        state = BETA * m_v[g] + t0 * g_v[g, 0].astype(F32)
        nm[g] = BETA * state + t1 * g_v[g, 1].astype(F32) - low
        return 0

    lax.fori_loop(0, 3, momentum_group, 0)

    owner = rep < PIECES

    @pl.when(owner)
    def _():
        rbuf[rep] = band[rep]
        drain(rbuf, REP - 1, None, r_recv)
        abuf[rep] = jnp.sum(rbuf[...], axis=0)

        def send_sum(d, _):
            pltpu.make_async_remote_copy(
                src_ref=abuf.at[rep], dst_ref=abuf.at[rep], send_sem=a_send, recv_sem=a_recv,
                device_id={"replica": lax.rem(rep + d, REP)}, device_id_type=MESH,
            ).start()
            return 0

        lax.fori_loop(1, REP, send_sum, 0)

    lax.fori_loop(3, GROUPS, momentum_group, 0)

    @pl.when(owner)
    def _():
        drain(rbuf, PIECES - 1, r_send, None)
        drain(rbuf, REP - 1, a_send, None)
        drain(abuf, PIECES - 1, None, a_recv)

    @pl.when(jnp.logical_not(owner))
    def _():
        drain(rbuf, PIECES, r_send, None)
        drain(abuf, PIECES, None, a_recv)

    summed[...] = abuf[...]


def write_kernel(nm, summed, wdec, ldec, out_m, out_u, upd, m_sem, u_sem):
    def m_copy(g, width):
        return pltpu.make_async_copy(nm.at[g, :, pl.ds(0, width)], out_m.at[0, :, pl.ds(g * GCOL, width)], m_sem.at[g])

    def u_copy(g, width):
        return pltpu.make_async_copy(upd.at[g, :, pl.ds(0, width)], out_u.at[:, pl.ds(g * GCOL, width)], u_sem.at[g])

    widths = [GCOL] * (GROUPS - 1) + [LAST]
    for g in range(GROUPS):
        m_copy(g, widths[g]).start()
    for g in range(GROUPS):
        piece = summed[pl.ds(4 * g, 4)].reshape(BROW, BCOL)
        upd[g] = decode_group(piece, wdec[...], ldec[...]).astype(BF16)
        u_copy(g, widths[g]).start()
    for g in range(GROUPS):
        m_copy(g, widths[g]).wait()
        u_copy(g, widths[g]).wait()


def per_device(momentum, grads):
    w_enc, l_enc, w_dec, l_dec = (jnp.asarray(t) for t in tables())
    hbm = pl.BlockSpec(memory_space=pl.ANY)
    vmem = pl.BlockSpec(memory_space=pltpu.VMEM)
    dma = pltpu.SemaphoreType.DMA
    nm, summed, wdec, ldec = pl.pallas_call(
        sync_kernel,
        out_shape=(
            pltpu.VMEM((GROUPS, ROWS, GCOL), F32),
            pltpu.VMEM((PIECES, QUART, BCOL), F32),
            pltpu.VMEM(w_dec.shape, BF16),
            pltpu.VMEM(l_dec.shape, BF16),
        ),
        in_specs=[hbm] * 6,
        out_specs=(vmem,) * 4,
        scratch_shapes=[
            pltpu.VMEM((GROUPS, ROWS, GCOL), F32),
            pltpu.VMEM((GROUPS, STEPS, ROWS, GCOL), BF16),
            pltpu.VMEM(w_enc.shape, BF16),
            pltpu.VMEM(l_enc.shape, BF16),
            pltpu.VMEM((GROUPS, STEPS + 1, BROW, BCOL), F32),
            pltpu.VMEM((PIECES, QUART, BCOL), F32),
            pltpu.VMEM((GROUPS, BROW, BCOL), F32),
            pltpu.VMEM((TEN, STEPS, 128), F32),
            pltpu.VMEM((REP, STEPS, 128), F32),
            pltpu.VMEM((REP, QUART, BCOL), F32),
            pltpu.VMEM((PIECES, QUART, BCOL), F32),
            pltpu.VMEM((STEPS, 128), F32),
            dma((GROUPS,)), dma((GROUPS,)), dma((4,)),
            dma, dma, dma, dma, dma, dma, dma, dma,
        ],
        compiler_params=pltpu.CompilerParams(
            collective_id=0, has_side_effects=True, vmem_limit_bytes=36 * 1024 * 1024
        ),
        name="sync",
    )(momentum, grads, w_enc, l_enc, w_dec, l_dec)
    return pl.pallas_call(
        write_kernel,
        out_shape=(
            jax.ShapeDtypeStruct((1, ROWS, COLS), F32),
            jax.ShapeDtypeStruct((ROWS, COLS), BF16),
        ),
        in_specs=[vmem] * 4,
        out_specs=(hbm, hbm),
        scratch_shapes=[pltpu.VMEM((GROUPS, ROWS, GCOL), BF16), dma((GROUPS,)), dma((GROUPS,))],
        compiler_params=pltpu.CompilerParams(vmem_limit_bytes=16 * 1024 * 1024),
        name="write",
    )(*(pltpu.with_memory_space_constraint(a, pltpu.VMEM) for a in (nm, summed, wdec, ldec)))


def solution(mesh):
    in_specs = (P("replica", None, "tensor"), P("replica", None, None, "tensor"))
    out_specs = (P("replica", None, "tensor"), P(None, "tensor"))
    return jax.shard_map(
        per_device, mesh=mesh, in_specs=in_specs, out_specs=out_specs, check_vma=False
    )
```

time: 347 us -> 49.8 us (0.14); the launches traced: 340 us -> 49.5 us
  waiting for transfers between devices: 133 us -> 0 us
  blocking collectives: 79.8 us -> 0 us
  matrix products: 73 us -> 0 us
  Pallas kernels: 0 us -> 41.2 us
  local copies, waits for them, and re-layouts: 26.8 us -> 7.68 us
  between operations: 15.8 us -> 0.65 us
  other arithmetic: 12.1 us -> 0 us
    psum x1 -> x0, waiting for transfers between devices: 132 us -> none  [per_device(): summed = lax.psum(band, 'replica')]
    psum x1 -> x0, blocking collectives: 79.8 us -> none  [per_device(): total = lax.psum(local_sq[step], ('replica', 'tensor'))]
    dot_general x12 -> x0, matrix products: 73 us -> none  [the longest x4 31.8 us: decode(): half = jnp.einsum('ln,akfl->akfn', low_band, blocks, precision=HIGH)]
    pallas_call x0 -> x2, Pallas kernels: none -> 41.2 us  [the longest x1 37.8 us: per_device(): pl.pallas_call(sync_kernel, out_shape=(pltpu.VMEM((GROUPS, ROWS, GCOL), F...]
    reshape x6 -> x0, local copies, waits for them, and re-layouts: 22.6 us -> none  [the longest x4 14.8 us: decode(): half = half.reshape(row_count // TILE, BAND, col_count)]
    sub x1 -> x0, other arithmetic: 5.46 us -> none  [per_device(): state = state - decode(band, low_band, row_count, col_count)]
    reduce_sum x1 -> x0, other arithmetic: 3.68 us -> none  [per_device(): jnp.sum(jnp.square(grads[0, step].astype(jnp.float32)))]
    unnamed x18 -> x12, local copies, waits for them, and re-layouts: 4.21 us -> 7.68 us
  transfers between devices with their start and end apart: 1 -> 0, of which waited for: 1 -> 0; matrix products, arithmetic and copies ran while one was open for 4% -> 0% of each run, Pallas kernels for 0% -> 0%
where the time goes in v1:
time: 49.8 us; the launch traced here: 49.5 us
  Pallas kernels  41.2 us (83%)
  local copies, waits for them, and re-layouts  7.68 us (15%)
  between operations  0.65 us (1%)
    pallas_call x1, Pallas kernels, per_device(): pl.pallas_call(sync_kernel, out_shape=(pltpu.VMEM((GROUPS, ROWS, GCOL), F...  37.8 us
    unnamed x12, local copies, waits for them, and re-layouts  7.68 us
    pallas_call x1, Pallas kernels, per_device(): pl.pallas_call(write_kernel, out_shape=(jax.ShapeDtypeStruct((1, ROWS, CO...  3.37 us

profile of v1, /device:TPU:32, one launch (start us, length us, event | category | flops | bytes accessed | tf_op | source)
XLA Modules:
  0.0 49.5 jit_solution(15879004113298402615)
XLA Ops:
  0.6 0.0 copy-start
  0.6 2.0 %copy-done = f32[1,256,3456]{2,1,0:T(8,128)S(1)} copy-done((f32[1,256,3456]{2,1,0:T(8,128)S(1)}, f32[1,256,3456]{2,1,0:T(8,128)}, u32[]{:S(2)}) %copy-start) | copy-done | bytes 3538968
  2.6 0.0 copy-start.1
  2.6 2.0 %copy-done.1 = bf16[1,2,256,3456]{3,2,1,0:T(8,128)(2,1)S(1)} copy-done((bf16[1,2,256,3456]{3,2,1,0:T(8,128)(2,1)S(1)}, bf16[1,2,256,3456]{3,2,1,0:T(8,128)(2,1)}, u32[]{:S(2)}) %copy-start.1) | copy-done | bytes 3538968
  4.6 0.0 copy-start.2
  4.6 1.0 %copy-done.2 = bf16[384,512]{1,0:T(8,128)(2,1)S(1)} copy-done((bf16[384,512]{1,0:T(8,128)(2,1)S(1)}, bf16[384,512]{1,0:T(8,128)(2,1)}, u32[]{:S(2)}) %copy-start.2) | copy-done | bytes 393240
  5.6 0.0 copy-start.3
  5.6 0.9 %copy-done.3 = bf16[512,256]{1,0:T(8,128)(2,1)S(1)} copy-done((bf16[512,256]{1,0:T(8,128)(2,1)S(1)}, bf16[512,256]{1,0:T(8,128)(2,1)}, u32[]{:S(2)}) %copy-start.3) | copy-done | bytes 262168
  6.6 0.0 copy-start.4
  6.6 0.9 %copy-done.4 = bf16[256,192]{1,0:T(8,128)(2,1)S(1)} copy-done((bf16[256,192]{1,0:T(8,128)(2,1)S(1)}, bf16[256,192]{1,0:T(8,128)(2,1)}, u32[]{:S(2)}) %copy-start.4) | copy-done | bytes 98328
  7.5 0.0 copy-start.5
  7.5 0.8 %copy-done.5 = bf16[128,256]{1,0:T(8,128)(2,1)S(1)} copy-done((bf16[128,256]{1,0:T(8,128)(2,1)S(1)}, bf16[128,256]{1,0:T(8,128)(2,1)}, u32[]{:S(2)}) %copy-start.5) | copy-done | bytes 65560
  8.3 37.8 %sync.1 = (f32[7,256,512]{2,1,0:T(8,128)S(1)}, f32[28,16,128]{2,1,0:T(8,128)S(1)}, bf16[384,512]{1,0:T(8,128)(2,1)S(1)}, bf16[256,192]{1,0:T(8,128)(2,1)S(1)}) custom-call(f32[1,256,3456]{2,1,0:T(8,128)S(1)} %copy-done, bf16[1,2,256,3456]{3,2,1,0:T(8,128)(2,1)S(1)} %copy-done.1, bf16[512,256]{1,0:T(8,128)(2,1)S(1)} %copy-done.3, ...), custom_call_target="tpu_custom_call" | custom-call | tf_op jit(solution)/shard_map/sync/pallas_call | solution.py:299
  46.2 3.4 %write.1 = (f32[1,256,3456]{2,1,0:T(8,128)}, bf16[256,3456]{1,0:T(8,128)(2,1)}) custom-call(f32[7,256,512]{2,1,0:T(8,128)S(1)} %get-tuple-element.6.nm, f32[28,16,128]{2,1,0:T(8,128)S(1)} %get-tuple-element.7.summed, bf16[384,512]{1,0:T(8,128)(2,1)S(1)} %get-tuple-element.8.wdec, bf16[256,192]{1,0:T(8,128)(2,1)S(1)} %get-tuple-element.9.ldec), custom_call_target="tpu_custom_call" | custom-call | tf_op jit(solution)/shard_map/write/pallas_call | solution.py:330
Async XLA Ops:
  0.6 2.0 %copy-start = (f32[1,256,3456]{2,1,0:T(8,128)S(1)}, f32[1,256,3456]{2,1,0:T(8,128)}, u32[]{:S(2)}) copy-start(f32[1,256,3456]{2,1,0:T(8,128)} %m_hbm.1) | copy-start | bytes 10616836
  2.6 2.0 %copy-start.1 = (bf16[1,2,256,3456]{3,2,1,0:T(8,128)(2,1)S(1)}, bf16[1,2,256,3456]{3,2,1,0:T(8,128)(2,1)}, u32[]{:S(2)}) copy-start(bf16[1,2,256,3456]{3,2,1,0:T(8,128)(2,1)} %g_hbm.1) | copy-start | bytes 10616836
  4.6 1.0 %copy-start.2 = (bf16[384,512]{1,0:T(8,128)(2,1)S(1)}, bf16[384,512]{1,0:T(8,128)(2,1)}, u32[]{:S(2)}) copy-start(bf16[384,512]{1,0:T(8,128)(2,1)} %constant.10.clone.wdec_hbm) | copy-start | bytes 1179652
  5.6 0.9 %copy-start.3 = (bf16[512,256]{1,0:T(8,128)(2,1)S(1)}, bf16[512,256]{1,0:T(8,128)(2,1)}, u32[]{:S(2)}) copy-start(bf16[512,256]{1,0:T(8,128)(2,1)} %constant.8.clone.wenc_hbm) | copy-start | bytes 786436
  6.6 0.9 %copy-start.4 = (bf16[256,192]{1,0:T(8,128)(2,1)S(1)}, bf16[256,192]{1,0:T(8,128)(2,1)}, u32[]{:S(2)}) copy-start(bf16[256,192]{1,0:T(8,128)(2,1)} %constant.11.clone.ldec_hbm) | copy-start | bytes 294916
  7.5 0.8 %copy-start.5 = (bf16[128,256]{1,0:T(8,128)(2,1)S(1)}, bf16[128,256]{1,0:T(8,128)(2,1)}, u32[]{:S(2)}) copy-start(bf16[128,256]{1,0:T(8,128)(2,1)} %constant.9.clone.lenc_hbm) | copy-start | bytes 196612

commit v2 on v1

v2 whole, which is shorter than its diff:
```python
import functools
import math

import jax
import jax.numpy as jnp
import ml_dtypes
import numpy as np
from jax import lax
from jax.experimental import pallas as pl
from jax.experimental.pallas import tpu as pltpu
from jax.sharding import PartitionSpec as P

TILE = 32
BAND = 8
STEPS = 2
BETA = 0.9
CLIP = 1.0
EPS = 1e-06

MESH = pl.DeviceIdType.MESH
F32 = jnp.float32
BF16 = jnp.bfloat16

REP = 32
TEN = 8
NX, NY, NZ, NC = 4, 4, 8, 2
PLANE = NX * NY * NC
ROWS = 256
COLS = 3456
GCOL = 512
GROUPS = 7
LAST = COLS - (GROUPS - 1) * GCOL
BROW = ROWS // TILE * BAND
BCOL = GCOL // TILE * BAND
QUART = 16
PIECES = GROUPS * (BROW // QUART)


def patterns():
    freq = np.arange(BAND, dtype=np.float64)[:, None]
    place = np.arange(TILE, dtype=np.float64)[None, :]
    weight = np.where(freq == 0, math.sqrt(1.0 / TILE), math.sqrt(2.0 / TILE))
    low = weight * np.cos(math.pi * (2.0 * place + 1.0) * freq / (2.0 * TILE))
    down = np.tile(low.T, (1, GCOL // BAND))
    across = np.tile(low, (1, GCOL // TILE))
    return np.concatenate([down, across], axis=0).astype(np.float32)


def block_diagonal(pattern, times, rows_per, cols_per):
    whole = jnp.concatenate([pattern] * times, axis=0)
    i = lax.broadcasted_iota(jnp.int32, whole.shape, 0) // rows_per
    j = lax.broadcasted_iota(jnp.int32, whole.shape, 1) // cols_per
    return halves(jnp.where(i == j, whole, 0.0))


def build_tables(pat, wenc, lenc, wdec, ldec):
    down, across = pat[:TILE], pat[TILE:]
    hi, lo = block_diagonal(down[:, :BCOL], GCOL // TILE, TILE, BAND)
    wenc[:, :BCOL] = hi
    wenc[:, BCOL:] = lo
    hi, lo = block_diagonal(across[:, :ROWS], ROWS // TILE, BAND, TILE)
    lenc[:BROW] = hi
    lenc[BROW:] = lo
    hi, lo = block_diagonal(across, GCOL // TILE, BAND, TILE)
    wdec[:BCOL] = hi
    wdec[BCOL:2 * BCOL] = hi
    wdec[2 * BCOL:] = lo
    hi, lo = block_diagonal(down[:, :BROW], ROWS // TILE, TILE, BAND)
    ldec[...] = jnp.concatenate([hi, hi, lo], axis=1)


def halves(a):
    hi = a.astype(BF16)
    return hi, (a - hi.astype(F32)).astype(BF16)


def dot(a, b):
    return jnp.dot(a, b, preferred_element_type=F32)


def decode_group(band, w_dec, l_dec):
    hi, lo = halves(band)
    wide = dot(jnp.concatenate([hi, lo, hi], axis=1), w_dec)
    hi, lo = halves(wide)
    return dot(l_dec, jnp.concatenate([hi, lo, hi], axis=0))


def far(k, n):
    return n // 2 + lax.div(k + 1, 2) * (1 - 2 * lax.rem(k, 2))


def drain(buf, count, sem):
    part = buf.at[pl.ds(0, count)]
    pltpu.make_async_copy(part, part, sem).wait()


def sync_kernel(
    m_hbm, g_hbm, pat_hbm,
    nm, upd,
    m_v, g_v, pat, wenc, lenc, wdec, ldec, xs, xr, zs, zr, abuf, sq1, sq2, scales,
    g_sem, m_sem, c_sem, p1_send, p1_recv, p2_send, p2_recv, x_send, x_recv, z_send, z_recv, a_send, a_recv,
):
    rep = lax.axis_index("replica")
    ten = lax.axis_index("tensor")
    z, x = lax.div(rep, NX), lax.rem(rep, NX)
    y, c = lax.div(ten, NC), lax.rem(ten, NC)

    def plane_peer(k):
        dx, dy, dc = far(lax.div(k, NY * NC), NX), far(lax.rem(lax.div(k, NC), NY), NY), far(lax.rem(k, NC), NC)
        return {
            "replica": z * NX + lax.rem(x + dx, NX),
            "tensor": lax.rem(y + dy, NY) * NC + lax.rem(c + dc, NC),
        }

    def z_peer(d):
        return {"replica": lax.rem(z + d, NZ) * NX + x}

    def x_peer(d):
        return {"replica": z * NX + lax.rem(x + d, NX)}

    def replica_peer(k):
        dz, dx = far(lax.div(k, NX), NZ), far(lax.rem(k, NX), NX)
        return {"replica": lax.rem(z + dz, NZ) * NX + lax.rem(x + dx, NX)}

    def send(src, dst, send_sem, recv_sem, peer):
        pltpu.make_async_remote_copy(
            src_ref=src, dst_ref=dst, send_sem=send_sem, recv_sem=recv_sem, device_id=peer, device_id_type=MESH
        ).start()

    def grad_copy(g, width):
        return pltpu.make_async_copy(
            g_hbm.at[0, :, :, pl.ds(g * GCOL, width)], g_v.at[g, :, :, pl.ds(0, width)], g_sem.at[g]
        )

    def mom_copy(g, width):
        return pltpu.make_async_copy(
            m_hbm.at[0, :, pl.ds(g * GCOL, width)], m_v.at[g, :, pl.ds(0, width)], m_sem.at[g]
        )

    widths = [GCOL] * (GROUPS - 1) + [LAST]
    for g in range(GROUPS):
        grad_copy(g, widths[g]).start()

    barrier = pltpu.get_barrier_semaphore()

    def greet_z(k, _):
        pl.semaphore_signal(barrier, inc=1, device_id=z_peer(far(k, NZ)), device_id_type=MESH)
        return 0

    def greet_plane(k, _):
        pl.semaphore_signal(barrier, inc=1, device_id=plane_peer(k), device_id_type=MESH)
        return 0

    lax.fori_loop(0, NZ - 1, greet_z, 0)
    lax.fori_loop(0, PLANE - 1, greet_plane, 0)

    pattern = pltpu.make_async_copy(pat_hbm, pat, c_sem)
    pattern.start()
    for g in range(GROUPS):
        mom_copy(g, widths[g]).start()
    pattern.wait()
    build_tables(pat, wenc, lenc, wdec, ldec)

    m_v[GROUPS - 1, :, LAST:] = jnp.zeros((ROWS, GCOL - LAST), F32)
    g_v[GROUPS - 1, :, :, LAST:] = jnp.zeros((STEPS, ROWS, GCOL - LAST), BF16)

    def squares(g, sums):
        def rows(i, sums):
            at = pl.ds(pl.multiple_of(i * 16, 16), 16)
            x0 = g_v[g, 0, at, :].astype(F32)
            x1 = g_v[g, 1, at, :].astype(F32)
            return sums[0] + x0 * x0, sums[1] + x1 * x1

        return lax.fori_loop(0, ROWS // 16, rows, sums, unroll=4)

    def waited(g, sums):
        grad_copy(g, GCOL).wait()
        return squares(g, sums)

    sums = (jnp.zeros((16, GCOL), F32), jnp.zeros((16, GCOL), F32))
    sums = lax.fori_loop(0, GROUPS - 1, waited, sums)
    grad_copy(GROUPS - 1, LAST).wait()
    sums = squares(GROUPS - 1, sums)

    def lanes(v):
        v = jnp.sum(v, axis=0, keepdims=True)
        return v[:, :128] + v[:, 128:256] + v[:, 256:384] + v[:, 384:]

    here = (x * NY + y) * NC + c
    sq1[here] = jnp.concatenate([lanes(sums[0]), lanes(sums[1])], axis=0)
    pl.semaphore_wait(barrier, NZ - 1 + PLANE - 1)

    def send_plane(k, _):
        send(sq1.at[here], sq1.at[here], p1_send, p1_recv, plane_peer(k))
        return 0

    lax.fori_loop(0, PLANE - 1, send_plane, 0)

    def encode_group(g):
        m_hi, m_lo = halves(m_v[g])
        w = wenc[...]
        cols = [dot(m_hi, w) + dot(m_lo, w)]
        for s in range(STEPS):
            cols.append(dot(g_v[g, s], w))
        wide = jnp.concatenate([v[:, :BCOL] + v[:, BCOL:] for v in cols], axis=1)
        hi, lo = halves(wide)
        first = dot(lenc[...], hi)
        e = first[:BROW] + first[BROW:] + dot(lenc[:BROW], lo)
        for i in range(STEPS + 1):
            xs[:, g, i] = e[:, i * BCOL:(i + 1) * BCOL].reshape(NX, QUART, BCOL)

    def send_quarters(g):
        for d in (2, 1, 3):
            send(xs.at[lax.rem(x + d, NX), g], xr.at[d - 1, g], x_send, x_recv, x_peer(d))

    def encode_waited(g, _):
        mom_copy(g, GCOL).wait()
        encode_group(g)
        send_quarters(g)
        return 0

    lax.fori_loop(0, GROUPS - 1, encode_waited, 0)
    mom_copy(GROUPS - 1, LAST).wait()
    encode_group(GROUPS - 1)
    send_quarters(GROUPS - 1)

    drain(sq1, PLANE - 1, p1_recv)
    sq2[z] = jnp.sum(sq1[...], axis=0)

    def send_z(k, _):
        send(sq2.at[z], sq2.at[z], p2_send, p2_recv, z_peer(far(k, NZ)))
        return 0

    lax.fori_loop(0, NZ - 1, send_z, 0)

    drain(xr, NX - 1, x_recv)
    mine = xs[x] + xr[0] + xr[1] + xr[2]

    drain(sq2, NZ - 1, p2_recv)
    total = jnp.sum(jnp.sum(sq2[...], axis=0), axis=1, keepdims=True)
    total = jnp.broadcast_to(total, (STEPS, 128))
    count = float(REP * ROWS * TEN * COLS)
    scale = jnp.minimum(1.0, CLIP / jnp.sqrt(total / count + EPS))
    scales[...] = scale
    s0, s1 = scale[0:1], scale[1:2]
    zs[...] = BETA * mine[:, 0] + s0 * mine[:, 1] + s1 * mine[:, 2]

    def send_group(k, _):
        d = far(k, NZ)
        peer = lax.rem(z + d, NZ)

        @pl.when(peer < GROUPS)
        def _():
            send(zs.at[peer], zr.at[d - 1], z_send, z_recv, z_peer(d))

        return 0

    lax.fori_loop(0, NZ - 1, send_group, 0)

    def momentum_group(g, _):
        sc = scales[...]
        t0, t1 = sc[0:1], sc[1:2]
        own = BETA * (BETA * xs[:, g, 0] + t0 * xs[:, g, 1]) + t1 * xs[:, g, 2]
        low = decode_group(own.reshape(BROW, BCOL), wdec[...], ldec[...])
        state = BETA * m_v[g] + t0[:, 0:1] * g_v[g, 0].astype(F32)
        nm[g] = BETA * state + t1[:, 0:1] * g_v[g, 1].astype(F32) - low
        return 0

    lax.fori_loop(0, 3, momentum_group, 0)

    owner = z < GROUPS

    @pl.when(owner)
    def _():
        drain(zr, NZ - 1, z_recv)
        abuf[rep] = zs[z] + jnp.sum(zr[...], axis=0)

        def send_sum(k, _):
            send(abuf.at[rep], abuf.at[rep], a_send, a_recv.at[z], replica_peer(k))
            return 0

        lax.fori_loop(0, REP - 1, send_sum, 0)

    lax.fori_loop(3, GROUPS, momentum_group, 0)

    def decode_sum(k, _):
        g = lax.rem(z + NZ + lax.div(k + 1, 2) * (2 * lax.rem(k, 2) - 1), NZ)

        @pl.when(g < GROUPS)
        def _():
            @pl.when(g == z)
            def _():
                drain(abuf, NX - 1, a_recv.at[g])

            @pl.when(g != z)
            def _():
                drain(abuf, NX, a_recv.at[g])

            piece = abuf[pl.ds(NX * g, NX)].reshape(BROW, BCOL)
            upd[g] = decode_group(piece, wdec[...], ldec[...]).astype(BF16)

        return 0

    lax.fori_loop(0, NZ, decode_sum, 0)

    drain(sq1, PLANE - 1, p1_send)
    drain(sq2, NZ - 1, p2_send)
    drain(xr, NX - 1, x_send)

    @pl.when(owner)
    def _():
        drain(zs, GROUPS - 1, z_send)
        drain(abuf, PIECES, a_send)
        drain(abuf, REP - 1 - PIECES, a_send)

    @pl.when(jnp.logical_not(owner))
    def _():
        drain(zs, GROUPS, z_send)


def write_kernel(nm, upd, out_m, out_u, m_sem, u_sem):
    copies = []
    for g in range(GROUPS):
        width = GCOL if g < GROUPS - 1 else LAST
        here, there = pl.ds(0, width), pl.ds(g * GCOL, width)
        copies.append(pltpu.make_async_copy(nm.at[g, :, here], out_m.at[0, :, there], m_sem.at[g]))
        copies.append(pltpu.make_async_copy(upd.at[g, :, here], out_u.at[:, there], u_sem.at[g]))
    for copy in copies:
        copy.start()
    for copy in copies:
        copy.wait()


def per_device(momentum, grads):
    table = jnp.asarray(patterns())
    hbm = pl.BlockSpec(memory_space=pl.ANY)
    vmem = pl.BlockSpec(memory_space=pltpu.VMEM)
    dma = pltpu.SemaphoreType.DMA
    nm, upd = pl.pallas_call(
        sync_kernel,
        out_shape=(
            pltpu.VMEM((GROUPS, ROWS, GCOL), F32),
            pltpu.VMEM((GROUPS, ROWS, GCOL), BF16),
        ),
        in_specs=[hbm] * 3,
        out_specs=(vmem,) * 2,
        scratch_shapes=[
            pltpu.VMEM((GROUPS, ROWS, GCOL), F32),
            pltpu.VMEM((GROUPS, STEPS, ROWS, GCOL), BF16),
            pltpu.VMEM((TILE + BAND, GCOL), F32),
            pltpu.VMEM((GCOL, 2 * BCOL), BF16),
            pltpu.VMEM((2 * BROW, ROWS), BF16),
            pltpu.VMEM((3 * BCOL, GCOL), BF16),
            pltpu.VMEM((ROWS, 3 * BROW), BF16),
            pltpu.VMEM((NX, GROUPS, STEPS + 1, QUART, BCOL), F32),
            pltpu.VMEM((NX - 1, GROUPS, STEPS + 1, QUART, BCOL), F32),
            pltpu.VMEM((GROUPS, QUART, BCOL), F32),
            pltpu.VMEM((NZ - 1, QUART, BCOL), F32),
            pltpu.VMEM((PIECES, QUART, BCOL), F32),
            pltpu.VMEM((PLANE, STEPS, 128), F32),
            pltpu.VMEM((NZ, STEPS, 128), F32),
            pltpu.VMEM((STEPS, 128), F32),
            dma((GROUPS,)), dma((GROUPS,)), dma,
            dma, dma, dma, dma, dma, dma, dma, dma, dma, dma((GROUPS,)),
        ],
        compiler_params=pltpu.CompilerParams(
            collective_id=0, has_side_effects=True, vmem_limit_bytes=36 * 1024 * 1024
        ),
        name="sync",
    )(*(pltpu.with_memory_space_constraint(a, pltpu.HBM) for a in (momentum, grads, table)))
    return pl.pallas_call(
        write_kernel,
        out_shape=(
            jax.ShapeDtypeStruct((1, ROWS, COLS), F32),
            jax.ShapeDtypeStruct((ROWS, COLS), BF16),
        ),
        in_specs=[vmem] * 2,
        out_specs=(hbm, hbm),
        scratch_shapes=[dma((GROUPS,)), dma((GROUPS,))],
        compiler_params=pltpu.CompilerParams(vmem_limit_bytes=8 * 1024 * 1024),
        name="write",
    )(*(pltpu.with_memory_space_constraint(a, pltpu.VMEM) for a in (nm, upd)))


def solution(mesh):
    in_specs = (P("replica", None, "tensor"), P("replica", None, None, "tensor"))
    out_specs = (P("replica", None, "tensor"), P(None, "tensor"))
    return jax.shard_map(
        per_device, mesh=mesh, in_specs=in_specs, out_specs=out_specs, check_vma=False
    )
```

time: 49.8 us -> 38.8 us (0.78); the launches traced: 49.5 us -> 38 us
  local copies, waits for them, and re-layouts: 7.68 us -> 0 us
  Pallas kernels: 41.2 us -> 37.4 us
    unnamed x12 -> x0, local copies, waits for them, and re-layouts: 7.68 us -> none
    pallas_call x1, Pallas kernels: 37.8 us -> 34.9 us  [per_device(): pl.pallas_call(sync_kernel, out_shape=(pltpu.VMEM((GROUPS, ROWS, GCOL), F...]
    pallas_call x1, Pallas kernels: 3.37 us -> 2.46 us  [per_device(): pl.pallas_call(write_kernel, out_shape=(jax.ShapeDtypeStruct((1, ROWS, CO...]
where the time goes in v2:
time: 38.8 us; the launch traced here: 38 us
  Pallas kernels  37.4 us (96%)
  between operations  0.64 us (2%)
    pallas_call x1, Pallas kernels, per_device(): pl.pallas_call(sync_kernel, out_shape=(pltpu.VMEM((GROUPS, ROWS, GCOL), F...  34.9 us
    pallas_call x1, Pallas kernels, per_device(): pl.pallas_call(write_kernel, out_shape=(jax.ShapeDtypeStruct((1, ROWS, CO...  2.46 us

profile of v2, /device:TPU:32, one launch (start us, length us, event | category | flops | bytes accessed | tf_op | source)
XLA Modules:
  0.0 38.0 jit_solution(216861824976381790)
XLA Ops:
  0.6 34.9 %sync.1 = (f32[7,256,512]{2,1,0:T(8,128)S(1)}, bf16[7,256,512]{2,1,0:T(8,128)(2,1)S(1)}) custom-call(f32[1,256,3456]{2,1,0:T(8,128)} %m_hbm.1, bf16[1,2,256,3456]{3,2,1,0:T(8,128)(2,1)} %g_hbm.1, f32[40,512]{1,0:T(8,128)} %constant.2.clone.pat_hbm), custom_call_target="tpu_custom_call" | custom-call | tf_op jit(solution)/shard_map/sync/pallas_call | solution.py:339
  35.6 2.5 %write.1 = (f32[1,256,3456]{2,1,0:T(8,128)}, bf16[256,3456]{1,0:T(8,128)(2,1)}) custom-call(f32[7,256,512]{2,1,0:T(8,128)S(1)} %get-tuple-element.4.nm, bf16[7,256,512]{2,1,0:T(8,128)(2,1)S(1)} %get-tuple-element.5.upd), custom_call_target="tpu_custom_call" | custom-call | tf_op jit(solution)/shard_map/write/pallas_call | solution.py:371

commit v3 on v2

--- a/solution.py
+++ b/solution.py
@@ -25,6 +25,7 @@
 TEN = 8
 NX, NY, NZ, NC = 4, 4, 8, 2
 PLANE = NX * NY * NC
+IDLE = 4
 ROWS = 256
 COLS = 3456
 GCOL = 512
@@ -53,7 +54,7 @@
     return halves(jnp.where(i == j, whole, 0.0))
 
 
-def build_tables(pat, wenc, lenc, wdec, ldec):
+def encode_tables(pat, wenc, lenc):
     down, across = pat[:TILE], pat[TILE:]
     hi, lo = block_diagonal(down[:, :BCOL], GCOL // TILE, TILE, BAND)
     wenc[:, :BCOL] = hi
@@ -61,6 +62,10 @@
     hi, lo = block_diagonal(across[:, :ROWS], ROWS // TILE, BAND, TILE)
     lenc[:BROW] = hi
     lenc[BROW:] = lo
+
+
+def decode_tables(pat, wdec, ldec):
+    down, across = pat[:TILE], pat[TILE:]
     hi, lo = block_diagonal(across, GCOL // TILE, BAND, TILE)
     wdec[:BCOL] = hi
     wdec[BCOL:2 * BCOL] = hi
@@ -85,6 +90,10 @@
     return dot(l_dec, jnp.concatenate([hi, lo, hi], axis=0))
 
 
+def group_of(plane):
+    return plane - lax.div(plane, IDLE + 1)
+
+
 def far(k, n):
     return n // 2 + lax.div(k + 1, 2) * (1 - 2 * lax.rem(k, 2))
 
@@ -97,7 +106,7 @@
 def sync_kernel(
     m_hbm, g_hbm, pat_hbm,
     nm, upd,
-    m_v, g_v, pat, wenc, lenc, wdec, ldec, xs, xr, zs, zr, abuf, sq1, sq2, scales,
+    m_v, g_v, pat, wenc, lenc, wdec, ldec, xs, xr, zs, zr, abuf, wide, sq1, sq2, scales,
     g_sem, m_sem, c_sem, p1_send, p1_recv, p2_send, p2_recv, x_send, x_recv, z_send, z_recv, a_send, a_recv,
 ):
     rep = lax.axis_index("replica")
@@ -137,6 +146,8 @@
             m_hbm.at[0, :, pl.ds(g * GCOL, width)], m_v.at[g, :, pl.ds(0, width)], m_sem.at[g]
         )
 
+    pattern = pltpu.make_async_copy(pat_hbm, pat, c_sem)
+    pattern.start()
     widths = [GCOL] * (GROUPS - 1) + [LAST]
     for g in range(GROUPS):
         grad_copy(g, widths[g]).start()
@@ -154,12 +165,8 @@
     lax.fori_loop(0, NZ - 1, greet_z, 0)
     lax.fori_loop(0, PLANE - 1, greet_plane, 0)
 
-    pattern = pltpu.make_async_copy(pat_hbm, pat, c_sem)
-    pattern.start()
-    for g in range(GROUPS):
-        mom_copy(g, widths[g]).start()
     pattern.wait()
-    build_tables(pat, wenc, lenc, wdec, ldec)
+    encode_tables(pat, wenc, lenc)
 
     m_v[GROUPS - 1, :, LAST:] = jnp.zeros((ROWS, GCOL - LAST), F32)
     g_v[GROUPS - 1, :, :, LAST:] = jnp.zeros((STEPS, ROWS, GCOL - LAST), BF16)
@@ -175,11 +182,13 @@
 
     def waited(g, sums):
         grad_copy(g, GCOL).wait()
+        mom_copy(g, GCOL).start()
         return squares(g, sums)
 
     sums = (jnp.zeros((16, GCOL), F32), jnp.zeros((16, GCOL), F32))
     sums = lax.fori_loop(0, GROUPS - 1, waited, sums)
     grad_copy(GROUPS - 1, LAST).wait()
+    mom_copy(GROUPS - 1, LAST).start()
     sums = squares(GROUPS - 1, sums)
 
     def lanes(v):
@@ -233,6 +242,8 @@
 
     lax.fori_loop(0, NZ - 1, send_z, 0)
 
+    decode_tables(pat, wdec, ldec)
+
     drain(xr, NX - 1, x_recv)
     mine = xs[x] + xr[0] + xr[1] + xr[2]
 
@@ -249,9 +260,9 @@
         d = far(k, NZ)
         peer = lax.rem(z + d, NZ)
 
-        @pl.when(peer < GROUPS)
+        @pl.when(peer != IDLE)
         def _():
-            send(zs.at[peer], zr.at[d - 1], z_send, z_recv, z_peer(d))
+            send(zs.at[group_of(peer)], zr.at[d - 1], z_send, z_recv, z_peer(d))
 
         return 0
 
@@ -268,40 +279,41 @@
 
     lax.fori_loop(0, 3, momentum_group, 0)
 
-    owner = z < GROUPS
+    owner = z != IDLE
+    mine_g = group_of(z)
 
     @pl.when(owner)
     def _():
         drain(zr, NZ - 1, z_recv)
-        abuf[rep] = zs[z] + jnp.sum(zr[...], axis=0)
+        own = abuf.at[mine_g * NX + x]
+        own[...] = zs[mine_g] + jnp.sum(zr[...], axis=0)
 
         def send_sum(k, _):
-            send(abuf.at[rep], abuf.at[rep], a_send, a_recv.at[z], replica_peer(k))
+            peer = lax.div(k, NX) * NX + lax.rem(x + lax.rem(k, NX), NX)
+
+            @pl.when(peer != rep)
+            def _():
+                send(own, own, a_send, a_recv, {"replica": peer})
+
             return 0
 
-        lax.fori_loop(0, REP - 1, send_sum, 0)
+        lax.fori_loop(0, REP, send_sum, 0)
 
     lax.fori_loop(3, GROUPS, momentum_group, 0)
 
-    def decode_sum(k, _):
-        g = lax.rem(z + NZ + lax.div(k + 1, 2) * (2 * lax.rem(k, 2) - 1), NZ)
-
-        @pl.when(g < GROUPS)
-        def _():
-            @pl.when(g == z)
-            def _():
-                drain(abuf, NX - 1, a_recv.at[g])
-
-            @pl.when(g != z)
-            def _():
-                drain(abuf, NX, a_recv.at[g])
-
-            piece = abuf[pl.ds(NX * g, NX)].reshape(BROW, BCOL)
-            upd[g] = decode_group(piece, wdec[...], ldec[...]).astype(BF16)
-
-        return 0
-
-    lax.fori_loop(0, NZ, decode_sum, 0)
+    @pl.when(owner)
+    def _():
+        drain(abuf, PIECES - 1, a_recv)
+
+    @pl.when(jnp.logical_not(owner))
+    def _():
+        drain(abuf, PIECES, a_recv)
+
+    hi, lo = halves(abuf[...].reshape(GROUPS * BROW, BCOL))
+    wide[...] = dot(jnp.concatenate([hi, lo, hi], axis=1), wdec[...])
+    for g in range(GROUPS):
+        hi, lo = halves(wide[g * BROW:(g + 1) * BROW])
+        upd[g] = dot(ldec[...], jnp.concatenate([hi, lo, hi], axis=0)).astype(BF16)
 
     drain(sq1, PLANE - 1, p1_send)
     drain(sq2, NZ - 1, p2_send)
@@ -357,11 +369,12 @@
             pltpu.VMEM((GROUPS, QUART, BCOL), F32),
             pltpu.VMEM((NZ - 1, QUART, BCOL), F32),
             pltpu.VMEM((PIECES, QUART, BCOL), F32),
+            pltpu.VMEM((GROUPS * BROW, GCOL), F32),
             pltpu.VMEM((PLANE, STEPS, 128), F32),
             pltpu.VMEM((NZ, STEPS, 128), F32),
             pltpu.VMEM((STEPS, 128), F32),
             dma((GROUPS,)), dma((GROUPS,)), dma,
-            dma, dma, dma, dma, dma, dma, dma, dma, dma, dma((GROUPS,)),
+            dma, dma, dma, dma, dma, dma, dma, dma, dma, dma,
         ],
         compiler_params=pltpu.CompilerParams(
             collective_id=0, has_side_effects=True, vmem_limit_bytes=36 * 1024 * 1024

time: 38.8 us -> 36 us (0.928); the launches traced: 38 us -> 35.9 us
  Pallas kernels: 37.4 us -> 35.3 us
    pallas_call x1, Pallas kernels: 34.9 us -> 32.8 us  [per_device(): pl.pallas_call(sync_kernel, out_shape=(pltpu.VMEM((GROUPS, ROWS, GCOL), F...]
where the time goes in v3:
time: 36 us; the launch traced here: 35.9 us
  Pallas kernels  35.3 us (98%)
  between operations  0.64 us (2%)
    pallas_call x1, Pallas kernels, per_device(): pl.pallas_call(sync_kernel, out_shape=(pltpu.VMEM((GROUPS, ROWS, GCOL), F...  32.8 us
    pallas_call x1, Pallas kernels, per_device(): pl.pallas_call(write_kernel, out_shape=(jax.ShapeDtypeStruct((1, ROWS, CO...  2.46 us

profile of v3, /device:TPU:32, one launch (start us, length us, event | category | flops | bytes accessed | tf_op | source)
XLA Modules:
  0.0 35.9 jit_solution(16791884069123014638)
XLA Ops:
  0.6 32.8 %sync.1 = (f32[7,256,512]{2,1,0:T(8,128)S(1)}, bf16[7,256,512]{2,1,0:T(8,128)(2,1)S(1)}) custom-call(f32[1,256,3456]{2,1,0:T(8,128)} %m_hbm.1, bf16[1,2,256,3456]{3,2,1,0:T(8,128)(2,1)} %g_hbm.1, f32[40,512]{1,0:T(8,128)} %constant.2.clone.pat_hbm), custom_call_target="tpu_custom_call" | custom-call | tf_op jit(solution)/shard_map/sync/pallas_call | solution.py:351
  33.5 2.5 %write.1 = (f32[1,256,3456]{2,1,0:T(8,128)}, bf16[256,3456]{1,0:T(8,128)(2,1)}) custom-call(f32[7,256,512]{2,1,0:T(8,128)S(1)} %get-tuple-element.4.nm, bf16[7,256,512]{2,1,0:T(8,128)(2,1)S(1)} %get-tuple-element.5.upd), custom_call_target="tpu_custom_call" | custom-call | tf_op jit(solution)/shard_map/write/pallas_call | solution.py:384

commit v4 on v3

--- a/solution.py
+++ b/solution.py
@@ -1,4 +1,4 @@
-import functools
+import itertools
 import math
 
 import jax
@@ -25,6 +25,7 @@
 TEN = 8
 NX, NY, NZ, NC = 4, 4, 8, 2
 PLANE = NX * NY * NC
+BEFORE = 3
 IDLE = 4
 ROWS = 256
 COLS = 3456
@@ -94,8 +95,12 @@
     return plane - lax.div(plane, IDLE + 1)
 
 
-def far(k, n):
-    return n // 2 + lax.div(k + 1, 2) * (1 - 2 * lax.rem(k, 2))
+def plane_of(group):
+    return group + lax.div(group, IDLE)
+
+
+def far(n):
+    return sorted(range(n), key=lambda d: -min(d, n - d))
 
 
 def drain(buf, count, sem):
@@ -114,22 +119,21 @@
     z, x = lax.div(rep, NX), lax.rem(rep, NX)
     y, c = lax.div(ten, NC), lax.rem(ten, NC)
 
-    def plane_peer(k):
-        dx, dy, dc = far(lax.div(k, NY * NC), NX), far(lax.rem(lax.div(k, NC), NY), NY), far(lax.rem(k, NC), NC)
-        return {
-            "replica": z * NX + lax.rem(x + dx, NX),
-            "tensor": lax.rem(y + dy, NY) * NC + lax.rem(c + dc, NC),
-        }
-
-    def z_peer(d):
-        return {"replica": lax.rem(z + d, NZ) * NX + x}
-
-    def x_peer(d):
-        return {"replica": z * NX + lax.rem(x + d, NX)}
-
-    def replica_peer(k):
-        dz, dx = far(lax.div(k, NX), NZ), far(lax.rem(k, NX), NX)
-        return {"replica": lax.rem(z + dz, NZ) * NX + lax.rem(x + dx, NX)}
+    zd = [lax.rem(z + d, NZ) for d in range(NZ)]
+    xd = [lax.rem(x + d, NX) for d in range(NX)]
+    yd = [lax.rem(y + d, NY) * NC for d in range(NY)]
+    cd = [c, 1 - c]
+    rows = z * NX
+    plane_peers = [
+        {"replica": rows + xd[dx], "tensor": yd[dy] + cd[dc]}
+        for dx, dy, dc in sorted(
+            itertools.product(range(NX), range(NY), range(NC)),
+            key=lambda d: -(min(d[0], NX - d[0]) + min(d[1], NY - d[1])),
+        )
+        if dx or dy or dc
+    ]
+    z_peers = {d: {"replica": zd[d] * NX + x} for d in range(1, NZ)}
+    x_peers = {d: {"replica": rows + xd[d]} for d in range(1, NX)}
 
     def send(src, dst, send_sem, recv_sem, peer):
         pltpu.make_async_remote_copy(
@@ -154,16 +158,9 @@
 
     barrier = pltpu.get_barrier_semaphore()
 
-    def greet_z(k, _):
-        pl.semaphore_signal(barrier, inc=1, device_id=z_peer(far(k, NZ)), device_id_type=MESH)
-        return 0
-
-    def greet_plane(k, _):
-        pl.semaphore_signal(barrier, inc=1, device_id=plane_peer(k), device_id_type=MESH)
-        return 0
-
-    lax.fori_loop(0, NZ - 1, greet_z, 0)
-    lax.fori_loop(0, PLANE - 1, greet_plane, 0)
+    greeted = [z_peers[d] for d in far(NZ)[:-1]]
+    for peer in plane_peers[:8] + greeted + plane_peers[8:]:
+        pl.semaphore_signal(barrier, inc=1, device_id=peer, device_id_type=MESH)
 
     pattern.wait()
     encode_tables(pat, wenc, lenc)
@@ -197,14 +194,6 @@
 
     here = (x * NY + y) * NC + c
     sq1[here] = jnp.concatenate([lanes(sums[0]), lanes(sums[1])], axis=0)
-    pl.semaphore_wait(barrier, NZ - 1 + PLANE - 1)
-
-    def send_plane(k, _):
-        send(sq1.at[here], sq1.at[here], p1_send, p1_recv, plane_peer(k))
-        return 0
-
-    lax.fori_loop(0, PLANE - 1, send_plane, 0)
-
     def encode_group(g):
         m_hi, m_lo = halves(m_v[g])
         w = wenc[...]
@@ -220,32 +209,67 @@
 
     def send_quarters(g):
         for d in (2, 1, 3):
-            send(xs.at[lax.rem(x + d, NX), g], xr.at[d - 1, g], x_send, x_recv, x_peer(d))
-
-    def encode_waited(g, _):
-        mom_copy(g, GCOL).wait()
+            send(xs.at[xd[d], g], xr.at[d - 1, g], x_send, x_recv.at[g], x_peers[d])
+
+    mine_g = group_of(z)
+
+    def turn(k):
+        return lax.rem(mine_g + 1 + k, GROUPS)
+
+    def encode_waited(k):
+        g = turn(k)
+
+        @pl.when(g < GROUPS - 1)
+        def _():
+            mom_copy(g, GCOL).wait()
+
+        @pl.when(g == GROUPS - 1)
+        def _():
+            mom_copy(GROUPS - 1, LAST).wait()
+
         encode_group(g)
-        send_quarters(g)
+        return g
+
+    def encode_send(k, _):
+        send_quarters(encode_waited(k))
         return 0
 
-    lax.fori_loop(0, GROUPS - 1, encode_waited, 0)
-    mom_copy(GROUPS - 1, LAST).wait()
-    encode_group(GROUPS - 1)
-    send_quarters(GROUPS - 1)
+    ready = encode_waited(0)
+
+    pl.semaphore_wait(barrier, NZ - 1 + PLANE - 1)
+
+    for peer in plane_peers:
+        send(sq1.at[here], sq1.at[here], p1_send, p1_recv, peer)
+
+    send_quarters(ready)
+    lax.fori_loop(1, GROUPS, encode_send, 0)
+
+    def relay(k, _):
+        g = turn(k)
+        part = xr.at[:, g]
+        pltpu.make_async_copy(part, part, x_recv.at[g]).wait()
+        zs[g] = xs[x, g] + xr[0, g] + xr[1, g] + xr[2, g]
+        plane = plane_of(g)
+
+        @pl.when(plane != z)
+        def _():
+            d = lax.rem(plane + NZ - z, NZ)
+            send(zs.at[g], zr.at[d - 1], z_send, z_recv, {"replica": plane * NX + x})
+
+        return 0
+
+    lax.fori_loop(0, BEFORE, relay, 0)
 
     drain(sq1, PLANE - 1, p1_recv)
     sq2[z] = jnp.sum(sq1[...], axis=0)
 
-    def send_z(k, _):
-        send(sq2.at[z], sq2.at[z], p2_send, p2_recv, z_peer(far(k, NZ)))
-        return 0
-
-    lax.fori_loop(0, NZ - 1, send_z, 0)
+    for d in far(NZ)[:-1]:
+        send(sq2.at[z], sq2.at[z], p2_send, p2_recv, z_peers[d])
+
 
     decode_tables(pat, wdec, ldec)
 
-    drain(xr, NX - 1, x_recv)
-    mine = xs[x] + xr[0] + xr[1] + xr[2]
+    lax.fori_loop(BEFORE, GROUPS, relay, 0)
 
     drain(sq2, NZ - 1, p2_recv)
     total = jnp.sum(jnp.sum(sq2[...], axis=0), axis=1, keepdims=True)
@@ -253,20 +277,6 @@
     count = float(REP * ROWS * TEN * COLS)
     scale = jnp.minimum(1.0, CLIP / jnp.sqrt(total / count + EPS))
     scales[...] = scale
-    s0, s1 = scale[0:1], scale[1:2]
-    zs[...] = BETA * mine[:, 0] + s0 * mine[:, 1] + s1 * mine[:, 2]
-
-    def send_group(k, _):
-        d = far(k, NZ)
-        peer = lax.rem(z + d, NZ)
-
-        @pl.when(peer != IDLE)
-        def _():
-            send(zs.at[group_of(peer)], zr.at[d - 1], z_send, z_recv, z_peer(d))
-
-        return 0
-
-    lax.fori_loop(0, NZ - 1, send_group, 0)
 
     def momentum_group(g, _):
         sc = scales[...]
@@ -277,29 +287,24 @@
         nm[g] = BETA * state + t1[:, 0:1] * g_v[g, 1].astype(F32) - low
         return 0
 
-    lax.fori_loop(0, 3, momentum_group, 0)
-
     owner = z != IDLE
-    mine_g = group_of(z)
 
     @pl.when(owner)
     def _():
         drain(zr, NZ - 1, z_recv)
         own = abuf.at[mine_g * NX + x]
-        own[...] = zs[mine_g] + jnp.sum(zr[...], axis=0)
-
-        def send_sum(k, _):
-            peer = lax.div(k, NX) * NX + lax.rem(x + lax.rem(k, NX), NX)
-
-            @pl.when(peer != rep)
+        whole = zs[mine_g] + jnp.sum(zr[...], axis=0)
+        own[...] = BETA * whole[0] + scale[0:1] * whole[1] + scale[1:2] * whole[2]
+
+        for plane in range(NZ):
+            for d in range(1, NX):
+                send(own, own, a_send, a_recv, {"replica": plane * NX + xd[d]})
+
+            @pl.when(plane != z)
             def _():
-                send(own, own, a_send, a_recv, {"replica": peer})
-
-            return 0
-
-        lax.fori_loop(0, REP, send_sum, 0)
-
-    lax.fori_loop(3, GROUPS, momentum_group, 0)
+                send(own, own, a_send, a_recv, {"replica": plane * NX + x})
+
+    lax.fori_loop(0, GROUPS, momentum_group, 0)
 
     @pl.when(owner)
     def _():
@@ -366,15 +371,15 @@
             pltpu.VMEM((ROWS, 3 * BROW), BF16),
             pltpu.VMEM((NX, GROUPS, STEPS + 1, QUART, BCOL), F32),
             pltpu.VMEM((NX - 1, GROUPS, STEPS + 1, QUART, BCOL), F32),
-            pltpu.VMEM((GROUPS, QUART, BCOL), F32),
-            pltpu.VMEM((NZ - 1, QUART, BCOL), F32),
+            pltpu.VMEM((GROUPS, STEPS + 1, QUART, BCOL), F32),
+            pltpu.VMEM((NZ - 1, STEPS + 1, QUART, BCOL), F32),
             pltpu.VMEM((PIECES, QUART, BCOL), F32),
             pltpu.VMEM((GROUPS * BROW, GCOL), F32),
             pltpu.VMEM((PLANE, STEPS, 128), F32),
             pltpu.VMEM((NZ, STEPS, 128), F32),
             pltpu.VMEM((STEPS, 128), F32),
             dma((GROUPS,)), dma((GROUPS,)), dma,
-            dma, dma, dma, dma, dma, dma, dma, dma, dma, dma,
+            dma, dma, dma, dma, dma, dma((GROUPS,)), dma, dma, dma, dma,
         ],
         compiler_params=pltpu.CompilerParams(
             collective_id=0, has_side_effects=True, vmem_limit_bytes=36 * 1024 * 1024

time: 36 us -> 34 us (0.944)
  Pallas kernels: 35.3 us -> 33 us
    pallas_call x1, Pallas kernels: 32.8 us -> 30.6 us  [per_device(): pl.pallas_call(sync_kernel, out_shape=(pltpu.VMEM((GROUPS, ROWS, GCOL), F...]
where the time goes in v4:
time: 34 us; the launch traced here: 33.7 us
  Pallas kernels  33 us (97%)
  between operations  0.64 us (2%)
    pallas_call x1, Pallas kernels, per_device(): pl.pallas_call(sync_kernel, out_shape=(pltpu.VMEM((GROUPS, ROWS, GCOL), F...  30.6 us
    pallas_call x1, Pallas kernels, per_device(): pl.pallas_call(write_kernel, out_shape=(jax.ShapeDtypeStruct((1, ROWS, CO...  2.46 us

profile of v4, /device:TPU:32, one launch (start us, length us, event | category | flops | bytes accessed | tf_op | source)
XLA Modules:
  0.0 33.7 jit_solution(15573686605651614397)
XLA Ops:
  0.6 30.6 %sync.1 = (f32[7,256,512]{2,1,0:T(8,128)S(1)}, bf16[7,256,512]{2,1,0:T(8,128)(2,1)S(1)}) custom-call(f32[1,256,3456]{2,1,0:T(8,128)} %m_hbm.1, bf16[1,2,256,3456]{3,2,1,0:T(8,128)(2,1)} %g_hbm.1, f32[40,512]{1,0:T(8,128)} %constant.2.clone.pat_hbm), custom_call_target="tpu_custom_call" | custom-call | tf_op jit(solution)/shard_map/sync/pallas_call | solution.py:356
  31.2 2.5 %write.1 = (f32[1,256,3456]{2,1,0:T(8,128)}, bf16[256,3456]{1,0:T(8,128)(2,1)}) custom-call(f32[7,256,512]{2,1,0:T(8,128)S(1)} %get-tuple-element.4.nm, bf16[7,256,512]{2,1,0:T(8,128)(2,1)S(1)} %get-tuple-element.5.upd), custom_call_target="tpu_custom_call" | custom-call | tf_op jit(solution)/shard_map/write/pallas_call | solution.py:389

commit v5 on v4

--- a/solution.py
+++ b/solution.py
@@ -25,6 +25,7 @@
 TEN = 8
 NX, NY, NZ, NC = 4, 4, 8, 2
 PLANE = NX * NY * NC
+BATCHES = ((0, 6, 5, 4), (1, 2, 3))
 BEFORE = 3
 IDLE = 4
 ROWS = 256
@@ -96,7 +97,7 @@
 
 
 def plane_of(group):
-    return group + lax.div(group, IDLE)
+    return group + group // IDLE
 
 
 def far(n):
@@ -153,14 +154,18 @@
     pattern = pltpu.make_async_copy(pat_hbm, pat, c_sem)
     pattern.start()
     widths = [GCOL] * (GROUPS - 1) + [LAST]
+    barrier = pltpu.get_barrier_semaphore()
+
+    greeted = [z_peers[d] for d in far(NZ)[:-1]]
+    greeted = plane_peers[:8] + greeted + plane_peers[8:]
+    for peer in greeted[:12]:
+        pl.semaphore_signal(barrier, inc=1, device_id=peer, device_id_type=MESH)
     for g in range(GROUPS):
         grad_copy(g, widths[g]).start()
 
-    barrier = pltpu.get_barrier_semaphore()
-
-    greeted = [z_peers[d] for d in far(NZ)[:-1]]
-    for peer in plane_peers[:8] + greeted + plane_peers[8:]:
+    for peer in greeted[12:]:
         pl.semaphore_signal(barrier, inc=1, device_id=peer, device_id_type=MESH)
+
 
     pattern.wait()
     encode_tables(pat, wenc, lenc)
@@ -237,11 +242,11 @@
     ready = encode_waited(0)
 
     pl.semaphore_wait(barrier, NZ - 1 + PLANE - 1)
+    send_quarters(ready)
 
     for peer in plane_peers:
         send(sq1.at[here], sq1.at[here], p1_send, p1_recv, peer)
 
-    send_quarters(ready)
     lax.fori_loop(1, GROUPS, encode_send, 0)
 
     def relay(k, _):
@@ -298,27 +303,32 @@
 
         for plane in range(NZ):
             for d in range(1, NX):
-                send(own, own, a_send, a_recv, {"replica": plane * NX + xd[d]})
+                send(own, own, a_send, a_recv.at[mine_g], {"replica": plane * NX + xd[d]})
 
             @pl.when(plane != z)
             def _():
-                send(own, own, a_send, a_recv, {"replica": plane * NX + x})
+                send(own, own, a_send, a_recv.at[mine_g], {"replica": plane * NX + x})
 
     lax.fori_loop(0, GROUPS, momentum_group, 0)
 
-    @pl.when(owner)
-    def _():
-        drain(abuf, PIECES - 1, a_recv)
-
-    @pl.when(jnp.logical_not(owner))
-    def _():
-        drain(abuf, PIECES, a_recv)
-
-    hi, lo = halves(abuf[...].reshape(GROUPS * BROW, BCOL))
-    wide[...] = dot(jnp.concatenate([hi, lo, hi], axis=1), wdec[...])
-    for g in range(GROUPS):
-        hi, lo = halves(wide[g * BROW:(g + 1) * BROW])
-        upd[g] = dot(ldec[...], jnp.concatenate([hi, lo, hi], axis=0)).astype(BF16)
+    def await_group(g):
+        @pl.when(plane_of(g) == z)
+        def _():
+            drain(abuf, NX - 1, a_recv.at[g])
+
+        @pl.when(plane_of(g) != z)
+        def _():
+            drain(abuf, NX, a_recv.at[g])
+
+    for batch in BATCHES:
+        for g in batch:
+            await_group(g)
+        parts = [abuf[g * NX:(g + 1) * NX].reshape(BROW, BCOL) for g in batch]
+        hi, lo = halves(jnp.concatenate(parts, axis=0))
+        wide[:len(batch) * BROW] = dot(jnp.concatenate([hi, lo, hi], axis=1), wdec[...])
+        for i, g in enumerate(batch):
+            hi, lo = halves(wide[i * BROW:(i + 1) * BROW])
+            upd[g] = dot(ldec[...], jnp.concatenate([hi, lo, hi], axis=0)).astype(BF16)
 
     drain(sq1, PLANE - 1, p1_send)
     drain(sq2, NZ - 1, p2_send)
@@ -379,7 +389,7 @@
             pltpu.VMEM((NZ, STEPS, 128), F32),
             pltpu.VMEM((STEPS, 128), F32),
             dma((GROUPS,)), dma((GROUPS,)), dma,
-            dma, dma, dma, dma, dma, dma((GROUPS,)), dma, dma, dma, dma,
+            dma, dma, dma, dma, dma, dma((GROUPS,)), dma, dma, dma, dma((GROUPS,)),
         ],
         compiler_params=pltpu.CompilerParams(
             collective_id=0, has_side_effects=True, vmem_limit_bytes=36 * 1024 * 1024

time: 34 us -> 33.8 us (level)
  no operation moved by 1% of the time
where the time goes in v5:
time: 33.8 us; the launch traced here: 33.5 us
  Pallas kernels  32.9 us (97%)
  between operations  0.64 us (2%)
    pallas_call x1, Pallas kernels, per_device(): pl.pallas_call(sync_kernel, out_shape=(pltpu.VMEM((GROUPS, ROWS, GCOL), F...  30.4 us
    pallas_call x1, Pallas kernels, per_device(): pl.pallas_call(write_kernel, out_shape=(jax.ShapeDtypeStruct((1, ROWS, CO...  2.46 us

profile of v5, /device:TPU:32, one launch (start us, length us, event | category | flops | bytes accessed | tf_op | source)
XLA Modules:
  0.0 33.5 jit_solution(10932403872622991347)
XLA Ops:
  0.6 30.4 %sync.1 = (f32[7,256,512]{2,1,0:T(8,128)S(1)}, bf16[7,256,512]{2,1,0:T(8,128)(2,1)S(1)}) custom-call(f32[1,256,3456]{2,1,0:T(8,128)} %m_hbm.1, bf16[1,2,256,3456]{3,2,1,0:T(8,128)(2,1)} %g_hbm.1, f32[40,512]{1,0:T(8,128)} %constant.2.clone.pat_hbm), custom_call_target="tpu_custom_call" | custom-call | tf_op jit(solution)/shard_map/sync/pallas_call | solution.py:366
  31.1 2.5 %write.1 = (f32[1,256,3456]{2,1,0:T(8,128)}, bf16[256,3456]{1,0:T(8,128)(2,1)}) custom-call(f32[7,256,512]{2,1,0:T(8,128)S(1)} %get-tuple-element.4.nm, bf16[7,256,512]{2,1,0:T(8,128)(2,1)S(1)} %get-tuple-element.5.upd), custom_call_target="tpu_custom_call" | custom-call | tf_op jit(solution)/shard_map/write/pallas_call | solution.py:399

commit v6 on v5

--- a/solution.py
+++ b/solution.py
@@ -180,7 +180,7 @@
             x1 = g_v[g, 1, at, :].astype(F32)
             return sums[0] + x0 * x0, sums[1] + x1 * x1
 
-        return lax.fori_loop(0, ROWS // 16, rows, sums, unroll=4)
+        return lax.fori_loop(0, ROWS // 16, rows, sums, unroll=16)
 
     def waited(g, sums):
         grad_copy(g, GCOL).wait()
@@ -276,6 +276,13 @@
 
     lax.fori_loop(BEFORE, GROUPS, relay, 0)
 
+    owner = z != IDLE
+
+    @pl.when(owner)
+    def _():
+        drain(zr, NZ - 1, z_recv)
+        zs[mine_g] = zs[mine_g] + jnp.sum(zr[...], axis=0)
+
     drain(sq2, NZ - 1, p2_recv)
     total = jnp.sum(jnp.sum(sq2[...], axis=0), axis=1, keepdims=True)
     total = jnp.broadcast_to(total, (STEPS, 128))
@@ -292,13 +299,10 @@
         nm[g] = BETA * state + t1[:, 0:1] * g_v[g, 1].astype(F32) - low
         return 0
 
-    owner = z != IDLE
-
     @pl.when(owner)
     def _():
-        drain(zr, NZ - 1, z_recv)
         own = abuf.at[mine_g * NX + x]
-        whole = zs[mine_g] + jnp.sum(zr[...], axis=0)
+        whole = zs[mine_g]
         own[...] = BETA * whole[0] + scale[0:1] * whole[1] + scale[1:2] * whole[2]
 
         for plane in range(NZ):

time: 33.8 us -> 33.9 us (level)
  no operation moved by 1% of the time
where the time goes in v6:
time: 33.9 us; the launch traced here: 33.6 us
  Pallas kernels  33 us (97%)
  between operations  0.64 us (2%)
    pallas_call x1, Pallas kernels, per_device(): pl.pallas_call(sync_kernel, out_shape=(pltpu.VMEM((GROUPS, ROWS, GCOL), F...  30.5 us
    pallas_call x1, Pallas kernels, per_device(): pl.pallas_call(write_kernel, out_shape=(jax.ShapeDtypeStruct((1, ROWS, CO...  2.46 us

profile of v6, /device:TPU:32, one launch (start us, length us, event | category | flops | bytes accessed | tf_op | source)
XLA Modules:
  0.0 33.6 jit_solution(13095434216647987134)
XLA Ops:
  0.6 30.5 %sync.1 = (f32[7,256,512]{2,1,0:T(8,128)S(1)}, bf16[7,256,512]{2,1,0:T(8,128)(2,1)S(1)}) custom-call(f32[1,256,3456]{2,1,0:T(8,128)} %m_hbm.1, bf16[1,2,256,3456]{3,2,1,0:T(8,128)(2,1)} %g_hbm.1, f32[40,512]{1,0:T(8,128)} %constant.2.clone.pat_hbm), custom_call_target="tpu_custom_call" | custom-call | tf_op jit(solution)/shard_map/sync/pallas_call | solution.py:370
  31.2 2.5 %write.1 = (f32[1,256,3456]{2,1,0:T(8,128)}, bf16[256,3456]{1,0:T(8,128)(2,1)}) custom-call(f32[7,256,512]{2,1,0:T(8,128)S(1)} %get-tuple-element.4.nm, bf16[7,256,512]{2,1,0:T(8,128)(2,1)S(1)} %get-tuple-element.5.upd), custom_call_target="tpu_custom_call" | custom-call | tf_op jit(solution)/shard_map/write/pallas_call | solution.py:403

commit v7 on v5

--- a/solution.py
+++ b/solution.py
@@ -26,7 +26,7 @@
 NX, NY, NZ, NC = 4, 4, 8, 2
 PLANE = NX * NY * NC
 BATCHES = ((0, 6, 5, 4), (1, 2, 3))
-BEFORE = 3
+BEFORE = 5
 IDLE = 4
 ROWS = 256
 COLS = 3456

time: 33.8 us -> 33.8 us (level)
  no operation moved by 1% of the time
where the time goes in v7:
time: 33.8 us; the launch traced here: 33.5 us
  Pallas kernels  32.8 us (97%)
  between operations  0.64 us (2%)
    pallas_call x1, Pallas kernels, per_device(): pl.pallas_call(sync_kernel, out_shape=(pltpu.VMEM((GROUPS, ROWS, GCOL), F...  30.4 us
    pallas_call x1, Pallas kernels, per_device(): pl.pallas_call(write_kernel, out_shape=(jax.ShapeDtypeStruct((1, ROWS, CO...  2.46 us

profile of v7, /device:TPU:32, one launch (start us, length us, event | category | flops | bytes accessed | tf_op | source)
XLA Modules:
  0.0 33.5 jit_solution(13445488822700854448)
XLA Ops:
  0.6 30.4 %sync.1 = (f32[7,256,512]{2,1,0:T(8,128)S(1)}, bf16[7,256,512]{2,1,0:T(8,128)(2,1)S(1)}) custom-call(f32[1,256,3456]{2,1,0:T(8,128)} %m_hbm.1, bf16[1,2,256,3456]{3,2,1,0:T(8,128)(2,1)} %g_hbm.1, f32[40,512]{1,0:T(8,128)} %constant.2.clone.pat_hbm), custom_call_target="tpu_custom_call" | custom-call | tf_op jit(solution)/shard_map/sync/pallas_call | solution.py:366
  31.0 2.5 %write.1 = (f32[1,256,3456]{2,1,0:T(8,128)}, bf16[256,3456]{1,0:T(8,128)(2,1)}) custom-call(f32[7,256,512]{2,1,0:T(8,128)S(1)} %get-tuple-element.4.nm, bf16[7,256,512]{2,1,0:T(8,128)(2,1)S(1)} %get-tuple-element.5.upd), custom_call_target="tpu_custom_call" | custom-call | tf_op jit(solution)/shard_map/write/pallas_call | solution.py:399
